TPU v7x, 32 devices: a whole 2x2x4 slice. The times are simulated.
32 devices in a mesh: gx: 8 (over y, x, core), gy: 4 (over z).
Axes of the slice: x: 2, y: 2, z: 4, core: 2. Of those that a mesh axis runs over, the one named last changes fastest.
Arguments:
- atmosphere_state: bfloat16 [128, 800, 1600], P('gy', 'gx'), may hold values from -6 to 6
- forcing: float32 [128], P('gy'), may hold values from -4 to 4
- mixing: float32 [4, 32, 32], replicated, may hold values from -1 to 1
- order_slot: int32 [800], replicated, may hold values from 0 to 799, each once
- legendre: bfloat16 [800, 800, 800], P('gx', None, 'gy'), may hold values from -0.21875 to 0.21875
- ocean_tracer: float32 [8, 256, 2048], P(None, 'gy', 'gx'), may hold values from -6 to 6
- kinetic: float32 [8, 256, 2048], P(None, 'gy', 'gx'), may hold values from 0.01 to 1
- dissipation: float32 [8, 256, 2048], P(None, 'gy', 'gx'), may hold values from 0.001 to 0.1
- wet_mask: int32 [256, 2048], P('gy', 'gx'), may hold values 0 or 1
- send_cell: int32 [4, 10240], P('gy', 'gx'), may hold values from 0 to 16383
- send_weight: float32 [4, 10240], P('gy', 'gx'), may hold values from 0.5 to 2
- receive_cell: int32 [4, 10240], P('gy', 'gx'), may hold values from 0 to 159999
- wind_source: int32 [4, 10240], P('gy', 'gx'), may hold values from 0 to 159999
- wind_target: int32 [4, 10240], P('gy', 'gx'), may hold values from 0 to 16383
- wind_count: int32 [4, 8, 8], P('gy', 'gx'), may hold values from 1 to 160, 640 in all within a row
Outputs:
- spectral: float32 [800, 800, 256], P('gx', 'gy')
- tracer_out: float32 [8, 256, 2048], P(None, 'gy', 'gx')
Inputs may be any that keep to these rules, and one draw needn't show every extreme that they name: `wind_count`: for every tile some band sends exactly 160 live slots.
All inputs are finite; a program needn't handle non-finite values. No bound on the sum of `wet_mask` on one device may be relied on, other than what follows from the above.
Results may differ from a plain program's by a relative error of at most 0.0035.
The roundings to bfloat16 on the way count: a program that leaves them out, or rounds other values in their place, can miss the bound.
Values may be sent and summed in bfloat16 or wider, within the bound.
A program may use at most 192 MiB of HBM per device.

v0:
```python
import math

import jax
import jax.numpy as jnp
from jax import lax
from jax.sharding import PartitionSpec as P

OSTEPS = 4


mix_coeff = 0.12
wind_coeff = 0.5


def with_halo(x, sides, width):
    for axis, dim in sides:
        peers, length = (lax.axis_size(axis), x.shape[dim])
        up = [(i, (i + 1) % peers) for i in range(peers - 1)]
        down = [(j, i) for i, j in up]
        last = lax.slice_in_dim(x, length - width, length, axis=dim)
        first = lax.slice_in_dim(x, 0, width, axis=dim)
        before = lax.ppermute(last, axis, up)
        after = lax.ppermute(first, axis, down)
        x = jnp.concatenate([before, x, after], axis=dim)
    return x


def order_table(order_slot, longitudes):
    lon_index = jnp.arange(longitudes, dtype=jnp.int32)
    phase = lon_index[:, None] * order_slot[None, :] % longitudes
    angle = phase.astype(jnp.float32) * (2.0 * math.pi / longitudes)
    scale = 1.0 / math.sqrt(longitudes)
    return jnp.stack([jnp.cos(angle) * scale, -jnp.sin(angle) * scale], axis=1).astype(jnp.bfloat16)


def relax(tracer, wetf, vface, padded):
    layers = tracer.shape[0]
    rows = tracer.shape[1]
    cols = tracer.shape[2]
    change = jnp.zeros_like(tracer)
    for row_shift, col_shift in ((0, 1), (2, 1), (1, 0), (1, 2)):
        nearby = padded[:, row_shift : row_shift + rows, col_shift : col_shift + cols]
        change = change + mix_coeff * wetf * nearby[layers] * (nearby[:layers] - tracer)
    flux = vface * (tracer[1:] - tracer[:-1])
    change = change.at[:-1].add(flux).at[1:].add(-flux)
    return tracer + change


def shards(
    atmosphere_state,
    forcing,
    mixing,
    order_slot,
    legendre,
    ocean_tracer,
    kinetic,
    dissipation,
    wet_mask,
    send_cell,
    send_weight,
    receive_cell,
    wind_source,
    wind_target,
    wind_count,
):
    bands = lax.axis_size("gx")
    field_rows, band_rows, longitudes = atmosphere_state.shape
    band_cells = band_rows * longitudes
    layers, tile_rows, tile_cols = ocean_tracer.shape
    tile_cells = tile_rows * tile_cols
    variables = mixing.shape[0]
    levels = mixing.shape[1]
    wetf = wet_mask.astype(jnp.float32)
    sea_top = (ocean_tracer[0] * wetf).reshape(tile_cells)
    offers = sea_top[send_cell.reshape(bands, -1)] * send_weight.reshape(bands, -1)
    arrived = lax.all_to_all(offers, "gx", split_axis=0, concat_axis=0, tiled=True)
    partial_surface = (
        jnp.zeros((band_cells,), jnp.float32).at[receive_cell.reshape(-1)].add(arrived.reshape(-1))
    )
    surface_fields = lax.psum(partial_surface, "gy").reshape(band_rows, longitudes)
    forced = (
        atmosphere_state.astype(jnp.float32) + forcing[:, None, None] * surface_fields[None]
    ).astype(jnp.bfloat16)
    offset = lax.axis_index("gy") * field_rows
    select = (jnp.arange(variables)[None, :] == jnp.arange(2)[:, None]).astype(jnp.float32)
    bottom = (select[:, :, None] * mixing[None, :, 0, :]).reshape(2, variables * levels)
    bottom_rows = lax.dynamic_slice_in_dim(bottom, offset, field_rows, 1)
    partial_wind_stress = jnp.dot(
        bottom_rows,
        forced.reshape(field_rows, band_cells).astype(jnp.float32),
        precision=lax.Precision.HIGHEST,
    )
    wind = lax.psum(partial_wind_stress.astype(jnp.bfloat16), "gy")
    orders = order_slot.shape[0]
    table = order_table(order_slot, longitudes).reshape(longitudes, 2 * orders)
    fourier = jnp.einsum("fal,lc->fca", forced, table, preferred_element_type=jnp.float32).astype(
        jnp.bfloat16
    )
    fourier = fourier.reshape(field_rows, 2, orders, band_rows)
    own_orders = legendre.shape[0]
    own_degrees = legendre.shape[2]
    my_orders = lax.dynamic_slice_in_dim(
        order_slot, lax.axis_index("gx") * own_orders, own_orders, 0
    )
    degree = lax.axis_index("gy") * own_degrees + jnp.arange(own_degrees, dtype=jnp.int32)
    masked = jnp.where(
        degree[None, None, :] >= my_orders[:, None, None], legendre, jnp.zeros_like(legendre)
    )
    moved = lax.all_to_all(fourier, "gx", split_axis=2, concat_axis=3, tiled=True)
    unmixed_values = jnp.einsum(
        "frsl,sln->snfr",
        lax.all_gather(moved, "gy", axis=0, tiled=True),
        masked,
        preferred_element_type=jnp.float32,
    )
    unmixed_values = unmixed_values.reshape(own_orders, own_degrees, variables, levels, 2)
    mixed_tracer = jnp.einsum(
        "hkz,fchzu->fchku", mixing, unmixed_values, precision=lax.Precision.HIGHEST
    )
    spectral = mixed_tracer.reshape(own_orders, own_degrees, variables * levels * 2)
    sources = wind_source.reshape(bands, -1)
    slots = sources.shape[1]
    every_band = lax.all_gather(wind, "gx", axis=1, tiled=True)
    global_cell = jnp.arange(bands, dtype=jnp.int32)[:, None] * band_cells + sources
    fetched = every_band[:, global_cell]
    live = (
        jnp.arange(slots, dtype=jnp.int32)[None, :] < wind_count.reshape(bands)[:, None]
    ).astype(jnp.float32)
    ocean_wind = (
        jnp.zeros((2, tile_cells), jnp.float32)
        .at[:, wind_target.reshape(-1)]
        .add((fetched.astype(jnp.float32) * live[None]).reshape(2, -1))
    )
    east_wind = ocean_wind[0].reshape(tile_rows, tile_cols)
    north_wind = ocean_wind[1].reshape(tile_rows, tile_cols)
    speed = east_wind**2 + north_wind**2
    energy = kinetic.at[0].add(wind_coeff * speed)
    ratio = 0.09 * energy * energy / dissipation
    viscosity = 0.25 * ratio / (1.0 + ratio)
    vface = 0.5 * (viscosity[:-1] + viscosity[1:]) * wetf[None]
    tracer = ocean_tracer
    for sub_step in range(OSTEPS):
        stacked = jnp.concatenate([tracer, wetf[None]], axis=0)
        padded = with_halo(stacked.astype(jnp.bfloat16), (("gx", 2), ("gy", 1)), 1).astype(
            stacked.dtype
        )
        tracer = relax(tracer, wetf, vface, padded)
    return (spectral, tracer)


def solution(mesh):
    placed = (
        P("gy", "gx", None),
        P("gy"),
        P(),
        P(),
        P("gx", None, "gy"),
        P(None, "gy", "gx"),
        P(None, "gy", "gx"),
        P(None, "gy", "gx"),
        P("gy", "gx"),
        P("gy", "gx"),
        P("gy", "gx"),
        P("gy", "gx"),
        P("gy", "gx"),
        P("gy", "gx"),
        P("gy", "gx", None),
    )
    return jax.shard_map(
        shards,
        mesh=mesh,
        in_specs=placed,
        out_specs=(P("gx", "gy", None), P(None, "gy", "gx")),
        check_vma=False,
    )
```

profile of v0, /device:TPU:0, one launch (start us, length us, event | category | flops | bytes accessed | tf_op | source)
XLA Modules:
  0.0 1347.2 jit_solution(9376767051227624562)
XLA Ops:
  13.8 25.7 %multiply_convert_fusion.1 = (bf16[1600,1,800]{0,2,1:T(8,128)(2,1)}, bf16[1600,1,800]{0,2,1:T(8,128)(2,1)}) fusion(s32[800]{0:T(1024)} %param.36), kind=kLoop, calls=%fused_computation.27 | loop fusion | flops 17920000 | bytes 5123200 | tf_op jit(solution)/shard_map/convert.9
  51.1 7.1 gather_fusion
  70.0 7.4 scatter_custom_fusion
  84.3 34.3 %all-reduce.3.cloned.1.call-done = f32[100,1600]{1,0:T(8,128)} async-done(((f32[100,1600]{1,0:T(8,128)}), f32[100,1600]{1,0:T(8,128)}) %all-reduce.3.cloned.1.call-update) | async-done | bytes 640016 | tf_op jit(solution)/shard_map/psum | solution.py:80
  118.6 7.3 add_convert_fusion
  129.9 10.4 copy.43
  140.3 12.5 reshape.658
  152.8 7.6 convolution_convert_fusion
  160.4 27.4 %fusion.10 = bf16[32,1600,100]{1,2,0:T(8,128)(2,1)} fusion(bf16[1600,1600,1]{0,1,2:T(8,128)(2,1)} %bitcast.130, bf16[32,100,1600]{2,0,1:T(8,128)(2,1)} %copy-done.2), kind=kOutput, calls=%fused_computation.16 | convolution fusion | flops 16389120000 | bytes 25600000 | tf_op jit(solution)/shard_map/fal,lc->fca/dot_general | solution.py:96
  187.8 18.5 %reshape.701 = bf16[32,2,800,100]{2,1,3,0:T(2,128)(2,1)} reshape(bf16[32,1600,100]{1,2,0:T(8,128)(2,1)} %fusion.10) | data formatting | bytes 20480000 | tf_op jit(solution)/shard_map/reshape | solution.py:99
  206.2 24.3 %copy.45 = bf16[32,2,800,100]{3,0,1,2:T(8,128)(2,1)} copy(bf16[32,2,800,100]{2,1,3,0:T(2,128)(2,1)} %reshape.701) | data formatting | bytes 20480000 | tf_op jit(solution)/shard_map/reshape | solution.py:99
  236.8 164.4 %all-to-all-done.1 = bf16[32,2,800,100]{3,0,1,2:T(8,128)(2,1)} async-done(((bf16[32,2,800,100]{3,0,1,2:T(8,128)(2,1)}), bf16[32,2,800,100]{3,0,1,2:T(8,128)(2,1)}, u32[]{:S(2)}, u32[]{:S(2)}) %all-to-all-start.1) | async-done | bytes 10240032 | tf_op jit(solution)/shard_map/all_to_all | solution.py:109
  401.2 29.0 %copy.68 = bf16[32,2,8,100,100]{4,2,0,1,3:T(8,128)(2,1)} copy(bf16[32,2,8,100,100]{4,0,1,3,2:T(8,128)(2,1)} %bitcast.7) | data formatting | bytes 20480000 | tf_op jit(solution)/shard_map/all_to_all | solution.py:109
  430.2 21.6 %all_to_all.21 = bf16[32,2,100,800]{3,0,1,2:T(8,128)(2,1)} reshape(bf16[32,2,100,8,100]{4,3,0,1,2:T(8,128)(2,1)} %bitcast.128) | data formatting | bytes 20480000 | tf_op jit(solution)/shard_map/all_to_all | solution.py:109
  453.1 11.3 gather_fusion.1
  465.0 12.3 scatter_custom_fusion.1
  477.3 10.6 fusion.13
  518.9 18.9 %collective-permute-done.11 = bf16[9,1,258]{2,1,0:T(2,128)(2,1)S(1)} collective-permute-done((bf16[9,1,258]{2,1,0:T(2,128)(2,1)S(1)}, bf16[9,1,258]{2,1,0:T(2,128)(2,1)S(1)}, u32[]{:S(2)}, u32[]{:S(2)}) %collective-permute-start.11) | collective-permute-done | bytes 4676 | tf_op jit(solution)/shard_map/ppermute | solution.py:23
  539.6 7.8 collective-permute-start.12
  560.5 653.8 %all-gather.3.cloned.1.call-done = bf16[128,2,100,800]{3,0,1,2:T(8,128)(2,1)} async-done(((bf16[32,2,100,800]{3,0,1,2:T(8,128)(2,1)}), bf16[128,2,100,800]{3,0,1,2:T(8,128)(2,1)}) %all-gather.3.cloned.1.call-update) | async-done | bytes 40960016 | tf_op jit(solution)/shard_map/all_gather | solution.py:112
  1214.3 37.5 %fusion = f32[100,200,128,2]{1,2,3,0:T(8,128)} fusion(bf16[128,2,100,800]{3,0,1,2:T(8,128)(2,1)} %all-gather.3.cloned.1.call-done, bf16[100,800,200]{1,2,0:T(8,128)(2,1)} %param.37, pred[100,200]{1,0:T(8,128)(4,1)S(1)} %broadcast_compare_fusion), kind=kOutput, calls=%fused_computation.5 | convolution fusion | flops 8208000000 | bytes 93460000 | tf_op jit(solution)/shard_map/frsl,sln->snfr/dot_general | solution.py:110
  1251.8 28.9 %fusion.7 = f32[100,200,4,32,2]{1,3,4,0,2:T(8,128)} fusion(f32[100,200,4,32,2]{1,3,2,4,0:T(8,128)} %bitcast.129, f32[4,32,32]{2,1,0:T(8,128)S(1)} %copy-done.7), kind=kOutput, calls=%fused_computation.15 | convolution fusion | flops 1966080000 | bytes 40976384 | tf_op jit(solution)/shard_map/hkz,fchzu->fchku/dot_general | solution.py:117
  1280.8 34.3 %copy.49 = f32[100,200,4,32,2]{0,1,4,3,2:T(8,128)} copy(f32[100,200,4,32,2]{1,3,4,0,2:T(8,128)} %fusion.7) | data formatting | bytes 40960000 | tf_op jit(solution)/shard_map/hkz,fchzu->fchku/transpose | solution.py:117
  1315.1 25.3 %copy.52 = f32[100,200,256]{2,1,0:T(8,128)} copy(f32[100,200,256]{0,1,2:T(8,128)} %bitcast.127) | data formatting | bytes 40960000
  (146 shorter events, 94.5 us)
Async XLA Ops:
  7.2 445.6 %copy-start = (s32[1,1,8]{2,1,0:T(1,128)S(1)}, s32[1,1,8]{2,1,0:T(1,128)}, u32[]{:S(2)}) copy-start(s32[1,1,8]{2,1,0:T(1,128)} %param.47) | copy-start | bytes 100
  9.3 30.9 %collective-permute-start = (bf16[9,64,1]{2,1,0:T(8,128)(2,1)S(1)}, bf16[9,64,1]{2,1,0:T(8,128)(2,1)S(1)}, u32[]{:S(2)}, u32[]{:S(2)}) collective-permute-start(bf16[9,64,1]{2,1,0:T(8,128)(2,1)S(1)} %get-tuple-element.154), channel_id=1, source_target_pairs={{0,4},{4,8},{8,12},{12,16},{16,20},{20,24},{24,28},{1,5},{5,9},{9,... | collective-permute-start | bytes 3464 | tf_op jit(solution)/shard_map/ppermute | solution.py:22
  11.7 28.6 %collective-permute-start.1 = (bf16[9,64,1]{2,1,0:T(8,128)(2,1)S(1)}, bf16[9,64,1]{2,1,0:T(8,128)(2,1)S(1)}, u32[]{:S(2)}, u32[]{:S(2)}) collective-permute-start(bf16[9,64,1]{2,1,0:T(8,128)(2,1)S(1)} %get-tuple-element.155), channel_id=1, source_target_pairs={{4,0},{8,4},{12,8},{16,12},{20,16},{24,20},{28,24},{5,1},{9,5},{13... | collective-permute-start | bytes 3464 | tf_op jit(solution)/shard_map/ppermute | solution.py:23
  40.6 5.8 collective-permute-start.2
  44.9 5.6 collective-permute-start.3
  58.9 11.0 all-to-all-start
  65.1 53.4 %all-reduce.3.cloned.1.call-start = ((), (), s32[]{:S(2)}) async-start(), calls=%async_computation.2 | async-start | bytes 1384448 | tf_op jit(solution)/shard_map/psum | solution.py:80
  78.5 157.6 %all-reduce.5.cloned.1.call-start = ((), (), s32[]{:S(2)}) async-start(), calls=%async_computation.4 | async-start | bytes 1280000 | tf_op jit(solution)/shard_map/psum | solution.py:93
  230.6 170.6 %all-to-all-start.1 = ((bf16[32,2,800,100]{3,0,1,2:T(8,128)(2,1)}), bf16[32,2,800,100]{3,0,1,2:T(8,128)(2,1)}, u32[]{:S(2)}, u32[]{:S(2)}) async-start(bf16[32,2,800,100]{3,0,1,2:T(8,128)(2,1)} %copy.45), calls=%async_computation.1 | async-start | bytes 26214400 | tf_op jit(solution)/shard_map/all_to_all | solution.py:109
  236.0 217.1 %all-gather.5.cloned.1.call-start = ((), (), s32[]{:S(2)}) async-start(), calls=%async_computation.5 | async-start | bytes 5760000 | tf_op jit(solution)/shard_map/all_gather | solution.py:123
  236.7 977.6 %all-gather.3.cloned.1.call-start = ((), (), s32[]{:S(2)}) async-start(), calls=%async_computation.3 | async-start | bytes 57344000 | tf_op jit(solution)/shard_map/all_gather | solution.py:112
  489.3 2.6 collective-permute-start.4
  490.6 3.4 collective-permute-start.5
  494.3 4.5 collective-permute-start.6
  497.3 5.9 collective-permute-start.7
  504.9 6.3 collective-permute-start.8
  509.9 3.3 collective-permute-start.9
  513.4 5.5 collective-permute-start.10
  517.5 20.4 %collective-permute-start.11 = (bf16[9,1,258]{2,1,0:T(2,128)(2,1)S(1)}, bf16[9,1,258]{2,1,0:T(2,128)(2,1)S(1)}, u32[]{:S(2)}, u32[]{:S(2)}) collective-permute-start(bf16[9,1,258]{2,1,0:T(2,128)(2,1)S(1)} %get-tuple-element.143), channel_id=1, source_target_pairs={{1,0},{2,1},{3,2},{5,4},{6,5},{7,6},{9,8},{10,9},{11,10},{13,12},{... | collective-permute-start | bytes 13940 | tf_op jit(solution)/shard_map/ppermute | solution.py:23
  539.6 9.9 collective-permute-start.12
  547.4 3.3 collective-permute-start.13
  551.0 2.8 collective-permute-start.14
  552.3 5.9 collective-permute-start.15
  560.5 691.3 %copy-start.7 = (f32[4,32,32]{2,1,0:T(8,128)S(1)}, f32[4,32,32]{2,1,0:T(8,128)}, u32[]{:S(2)}) copy-start(f32[4,32,32]{2,1,0:T(8,128)} %param.35) | copy-start | bytes 49156
  (10 other events, 239.4 us)
Sparse Core Ops, SparseCore 0:
  78.6 39.9 all-reduce.2
  160.5 40.1 all-reduce.4
  238.7 107.8 all-gather.4
  451.9 762.3 all-gather.2
where the time goes:
time: 1360 us; the launch traced here: 1350 us
  waiting for transfers between devices  895 us (66%)
  local copies, waits for them, and re-layouts  203 us (15%)
  matrix products  101 us (7%)
  other arithmetic  82.1 us (6%)
  starting transfers between devices  51.2 us (4%)
  between operations  14.6 us (1%)
    all_gather x1, waiting for transfers between devices, shards(): lax.all_gather(moved, 'gy', axis=0, tiled=True)  654 us
    all_to_all x1, waiting for transfers between devices, shards(): lax.all_to_all(fourier, 'gx', split_axis=2, concat_axis=3, tiled=True)  164 us
    all_to_all x2, local copies, waits for them, and re-layouts, shards(): lax.all_to_all(fourier, 'gx', split_axis=2, concat_axis=3, tiled=True)  50.6 us
    reshape x2, local copies, waits for them, and re-layouts, shards(): fourier = fourier.reshape(field_rows, 2, orders, band_rows)  42.8 us
    dot_general x1, matrix products, shards(): jnp.einsum('frsl,sln->snfr', lax.all_gather(moved, 'gy', axis=0, tiled=Tr...  37.5 us
    ppermute x8, waiting for transfers between devices, with_halo(): after = lax.ppermute(first, axis, down)  37.1 us
    transpose x1, local copies, waits for them, and re-layouts, shards(): jnp.einsum('hkz,fchzu->fchku', mixing, unmixed_values, precision=lax.Prec...  34.3 us
    psum x1, waiting for transfers between devices, shards(): lax.psum(partial_surface, 'gy').reshape(band_rows, longitudes)  34.3 us
  transfers between devices with their start and end apart: 22, of which 14 were waited for; matrix products, arithmetic and copies ran while one was open for 13% of the time, Pallas kernels for 0%

commit v1 on v0

--- a/solution.py
+++ b/solution.py
@@ -1,8 +1,11 @@
+import functools
 import math
 
 import jax
 import jax.numpy as jnp
 from jax import lax
+from jax.experimental import pallas as pl
+from jax.experimental.pallas import tpu as pltpu
 from jax.sharding import PartitionSpec as P
 
 OSTEPS = 4
@@ -26,11 +29,21 @@
 
 
 def order_table(order_slot, longitudes):
-    lon_index = jnp.arange(longitudes, dtype=jnp.int32)
-    phase = lon_index[:, None] * order_slot[None, :] % longitudes
-    angle = phase.astype(jnp.float32) * (2.0 * math.pi / longitudes)
+    product = jnp.arange(longitudes, dtype=jnp.float32)[:, None] * order_slot.astype(jnp.float32)[None, :]
+    k = product - longitudes * jnp.round(product * (1.0 / longitudes))
+    x = (jnp.abs(k) * (2.0 / longitudes) - 0.5) * math.pi
+    y = x * x
     scale = 1.0 / math.sqrt(longitudes)
-    return jnp.stack([jnp.cos(angle) * scale, -jnp.sin(angle) * scale], axis=1).astype(jnp.bfloat16)
+    sine = sum_series(y, [(-1) ** i * scale / math.factorial(2 * i + 1) for i in range(7)]) * x
+    cosine = sum_series(y, [(-1) ** i * scale / math.factorial(2 * i) for i in range(8)])
+    return (-sine).astype(jnp.bfloat16), jnp.where(k < 0, cosine, -cosine).astype(jnp.bfloat16)
+
+
+def sum_series(y, terms):
+    total = jnp.full_like(y, terms[-1])
+    for term in terms[-2::-1]:
+        total = total * y + term
+    return total
 
 
 def relax(tracer, wetf, vface, padded):
@@ -44,6 +57,291 @@
     flux = vface * (tracer[1:] - tracer[:-1])
     change = change.at[:-1].add(flux).at[1:].add(-flux)
     return tracer + change
+
+
+PAIRS = 4
+LAG = 2
+AHEAD = 3
+MESH = pl.DeviceIdType.MESH
+
+
+def spectral_kernel(
+    nx, nz, chunks, four_ref, leg_ref, mix_ref, order_ref, out_ref,
+    held, legs, outs, own_sem, a_send, a_recv, z_send, z_recv, leg_sem, out_sem,
+):
+    me_x = lax.axis_index("gx")
+    me_z = lax.axis_index("gy")
+    own_orders, lats, degrees = leg_ref.shape
+    band = lats // nx
+    per_chunk = 2 * PAIRS
+
+    barrier = pltpu.get_barrier_semaphore()
+    for d in range(1, nx):
+        pl.semaphore_signal(
+            barrier, inc=1, device_id=(lax.rem(me_x + d, nx), me_z), device_id_type=MESH
+        )
+
+    @pl.when(me_z > 0)
+    def _():
+        pl.semaphore_signal(barrier, inc=1, device_id=(me_x, me_z - 1), device_id_type=MESH)
+
+    @pl.when(me_z < nz - 1)
+    def _():
+        pl.semaphore_signal(barrier, inc=1, device_id=(me_x, me_z + 1), device_id_type=MESH)
+
+    beside = jnp.where(me_z > 0, 1, 0) + jnp.where(me_z < nz - 1, 1, 0)
+    pl.semaphore_wait(barrier, nx - 1 + beside)
+
+    def own_copy(c):
+        return pltpu.make_async_copy(
+            four_ref.at[me_x, c], held.at[c, me_z, me_x], own_sem.at[c]
+        )
+
+    def band_copy(c, d):
+        peer = lax.rem(me_x + d, nx)
+        return pltpu.make_async_remote_copy(
+            src_ref=four_ref.at[peer, c],
+            dst_ref=held.at[c, me_z, me_x],
+            send_sem=a_send.at[c, d],
+            recv_sem=a_recv.at[c, d],
+            device_id=(peer, me_z),
+            device_id_type=MESH,
+        )
+
+    def group_copy(way, hop, c):
+        step = 1 if way == 0 else -1
+        group = me_z - step * hop
+        return pltpu.make_async_remote_copy(
+            src_ref=held.at[c, group],
+            dst_ref=held.at[c, group],
+            send_sem=z_send.at[way, hop, c],
+            recv_sem=z_recv.at[way, hop, c],
+            device_id=(me_x, me_z + step),
+            device_id_type=MESH,
+        )
+
+    def arrived(way, hop, c):
+        step = 1 if way == 0 else -1
+        group = me_z - step * (hop + 1)
+        pltpu.make_async_copy(
+            held.at[c, group], held.at[c, group], z_recv.at[way, hop, c]
+        ).wait()
+
+    def leg_copy(s, slot):
+        return pltpu.make_async_copy(leg_ref.at[s], legs.at[slot], leg_sem.at[slot])
+
+    def out_copy(s, slot):
+        return pltpu.make_async_copy(outs.at[slot], out_ref.at[s], out_sem.at[slot])
+
+    def send_bands(c):
+        own_copy(c).start()
+        for d in range(1, nx):
+            band_copy(c, d).start()
+
+    leg_copy(0, 0).start()
+    for c in range(min(AHEAD, chunks)):
+        send_bands(c)
+
+    def contract(c):
+        for q in range(PAIRS):
+            rows = slice(q * band, (q + 1) * band)
+
+            def one_order(s2, carry):
+                s = c * per_chunk + 2 * q + s2
+
+                @pl.when(s < own_orders)
+                def _():
+                    leg_copy(s, s2).wait()
+
+                    @pl.when(s + 1 < own_orders)
+                    def _():
+                        leg_copy(s + 1, 1 - s2).start()
+
+                    raw = jnp.zeros((degrees, nz * 128), jnp.float32)
+                    for b in range(nx):
+                        block = jnp.concatenate(
+                            [held[c, g, b, rows, :] for g in range(nz)], axis=1
+                        )
+                        raw = raw + lax.dot_general(
+                            legs[s2, b * band : (b + 1) * band, :],
+                            block,
+                            (((0,), (0,)), ((), ())),
+                            preferred_element_type=jnp.float32,
+                        )
+                    degree = me_z * degrees + lax.broadcasted_iota(jnp.int32, raw.shape, 0)
+                    raw = jnp.where(degree >= order_ref[me_x * own_orders + s], raw, 0.0)
+
+                    @pl.when(s >= 2)
+                    def _():
+                        out_copy(s - 2, s2).wait()
+
+                    outs[s2] = jnp.dot(
+                        raw,
+                        mix_ref[s2],
+                        precision=lax.Precision.HIGHEST,
+                        preferred_element_type=jnp.float32,
+                    )
+                    out_copy(s, s2).start()
+
+                return carry
+
+            lax.fori_loop(0, 2, one_order, 0)
+
+    def step(t, carry):
+        @pl.when(t + AHEAD < chunks)
+        def _():
+            send_bands(t + AHEAD)
+
+        @pl.when(t < chunks)
+        def _():
+            own_copy(t).wait()
+            for d in range(1, nx):
+                band_copy(t, d).wait_recv()
+
+            @pl.when(me_z < nz - 1)
+            def _():
+                group_copy(0, 0, t).start()
+
+            @pl.when(me_z > 0)
+            def _():
+                group_copy(1, 0, t).start()
+
+        for hop in range(1, nz):
+            c = t - LAG * hop
+
+            @pl.when((c >= 0) & (c < chunks))
+            def _():
+                @pl.when(me_z >= hop)
+                def _():
+                    arrived(0, hop - 1, c)
+                    if hop < nz - 1:
+
+                        @pl.when(me_z < nz - 1)
+                        def _():
+                            group_copy(0, hop, c).start()
+
+                @pl.when(me_z < nz - hop)
+                def _():
+                    arrived(1, hop - 1, c)
+                    if hop < nz - 1:
+
+                        @pl.when(me_z > 0)
+                        def _():
+                            group_copy(1, hop, c).start()
+
+        last = t - LAG * (nz - 1)
+
+        @pl.when(last >= 0)
+        def _():
+            contract(last)
+
+        return carry
+
+    lax.fori_loop(0, chunks + LAG * (nz - 1), step, 0)
+
+    out_copy(own_orders - 2, (own_orders - 2) % 2).wait()
+    out_copy(own_orders - 1, (own_orders - 1) % 2).wait()
+
+    def finish(c, carry):
+        for d in range(1, nx):
+            band_copy(c, d).wait_send()
+        for hop in range(nz - 1):
+
+            @pl.when((me_z >= hop) & (me_z < nz - 1))
+            def _():
+                group_copy(0, hop, c).wait_send()
+
+            @pl.when((me_z < nz - hop) & (me_z > 0))
+            def _():
+                group_copy(1, hop, c).wait_send()
+
+        return carry
+
+    lax.fori_loop(0, chunks, finish, 0)
+
+
+def spectral_part(forced, mixing, order_slot, legendre):
+    nx, nz = lax.axis_size("gx"), lax.axis_size("gy")
+    field_rows, band, longitudes = forced.shape
+    own_orders, lats, degrees = legendre.shape
+    variables, levels = mixing.shape[:2]
+    fields = variables * levels
+    if field_rows * 4 != 128 or (PAIRS * band) % 16 or own_orders % 2:
+        return spectral_plain(forced, mixing, order_slot, legendre)
+    chunks = -(-own_orders // (2 * PAIRS))
+    padded = chunks * 2 * PAIRS
+    slots = jnp.pad(order_slot.reshape(nx, own_orders), ((0, 0), (0, padded - own_orders)))
+    pairs = nx * padded // 2
+    cosine, sine = order_table(slots.reshape(pairs, 2).T.reshape(-1), longitudes)
+    table = jnp.stack([cosine.reshape(longitudes, 2, pairs), sine.reshape(longitudes, 2, pairs)], 2)
+    four = jnp.einsum(
+        "fal,lqp->paqf", forced, table.reshape(longitudes, 4, pairs), preferred_element_type=jnp.float32
+    ).astype(jnp.bfloat16)
+    four = four.reshape(nx, chunks, PAIRS * band, 128)
+    mix = mixing[:, None, :, :, None] * jnp.eye(variables, dtype=mixing.dtype)[:, :, None, None, None]
+    mix = mix.transpose(1, 3, 0, 2, 4).reshape(nz, 1, field_rows, fields, 1)
+    mix = mix[:, :, None] * jnp.eye(2, dtype=mixing.dtype)[None, None, :, None, None, :]
+    mix = jnp.eye(2, dtype=mixing.dtype)[:, None, :, None, None, None, None] * mix[None]
+    mix = mix.reshape(2, nz * 128, fields * 2)
+    scratch = [
+        pltpu.VMEM((chunks, nz, nx, PAIRS * band, 128), jnp.bfloat16),
+        pltpu.VMEM((2, lats, degrees), legendre.dtype),
+        pltpu.VMEM((2, degrees, 2 * fields), jnp.float32),
+        pltpu.SemaphoreType.DMA((chunks,)),
+        pltpu.SemaphoreType.DMA((chunks, nx)),
+        pltpu.SemaphoreType.DMA((chunks, nx)),
+        pltpu.SemaphoreType.DMA((2, nz - 1, chunks)),
+        pltpu.SemaphoreType.DMA((2, nz - 1, chunks)),
+        pltpu.SemaphoreType.DMA((2,)),
+        pltpu.SemaphoreType.DMA((2,)),
+    ]
+    return pl.pallas_call(
+        functools.partial(spectral_kernel, nx, nz, chunks),
+        out_shape=jax.ShapeDtypeStruct((own_orders, degrees, 2 * fields), jnp.float32),
+        in_specs=[
+            pl.BlockSpec(memory_space=pl.ANY),
+            pl.BlockSpec(memory_space=pl.ANY),
+            pl.BlockSpec(memory_space=pltpu.VMEM),
+            pl.BlockSpec(memory_space=pltpu.SMEM),
+        ],
+        out_specs=pl.BlockSpec(memory_space=pl.ANY),
+        scratch_shapes=scratch,
+        compiler_params=pltpu.CompilerParams(
+            collective_id=0, has_side_effects=True, vmem_limit_bytes=58 << 20
+        ),
+    )(four, legendre, mix, order_slot)
+
+
+def spectral_plain(forced, mixing, order_slot, legendre):
+    field_rows, band_rows, longitudes = forced.shape
+    variables, levels = mixing.shape[:2]
+    orders = order_slot.shape[0]
+    table = jnp.stack(order_table(order_slot, longitudes), axis=1).reshape(longitudes, 2 * orders)
+    fourier = jnp.einsum("fal,lc->fca", forced, table, preferred_element_type=jnp.float32).astype(
+        jnp.bfloat16
+    )
+    fourier = fourier.reshape(field_rows, 2, orders, band_rows)
+    own_orders = legendre.shape[0]
+    own_degrees = legendre.shape[2]
+    my_orders = lax.dynamic_slice_in_dim(
+        order_slot, lax.axis_index("gx") * own_orders, own_orders, 0
+    )
+    degree = lax.axis_index("gy") * own_degrees + jnp.arange(own_degrees, dtype=jnp.int32)
+    masked = jnp.where(
+        degree[None, None, :] >= my_orders[:, None, None], legendre, jnp.zeros_like(legendre)
+    )
+    moved = lax.all_to_all(fourier, "gx", split_axis=2, concat_axis=3, tiled=True)
+    unmixed_values = jnp.einsum(
+        "frsl,sln->snfr",
+        lax.all_gather(moved, "gy", axis=0, tiled=True),
+        masked,
+        preferred_element_type=jnp.float32,
+    )
+    unmixed_values = unmixed_values.reshape(own_orders, own_degrees, variables, levels, 2)
+    mixed_tracer = jnp.einsum(
+        "hkz,fchzu->fchku", mixing, unmixed_values, precision=lax.Precision.HIGHEST
+    )
+    return mixed_tracer.reshape(own_orders, own_degrees, variables * levels * 2)
 
 
 def shards(
@@ -91,33 +389,7 @@
         precision=lax.Precision.HIGHEST,
     )
     wind = lax.psum(partial_wind_stress.astype(jnp.bfloat16), "gy")
-    orders = order_slot.shape[0]
-    table = order_table(order_slot, longitudes).reshape(longitudes, 2 * orders)
-    fourier = jnp.einsum("fal,lc->fca", forced, table, preferred_element_type=jnp.float32).astype(
-        jnp.bfloat16
-    )
-    fourier = fourier.reshape(field_rows, 2, orders, band_rows)
-    own_orders = legendre.shape[0]
-    own_degrees = legendre.shape[2]
-    my_orders = lax.dynamic_slice_in_dim(
-        order_slot, lax.axis_index("gx") * own_orders, own_orders, 0
-    )
-    degree = lax.axis_index("gy") * own_degrees + jnp.arange(own_degrees, dtype=jnp.int32)
-    masked = jnp.where(
-        degree[None, None, :] >= my_orders[:, None, None], legendre, jnp.zeros_like(legendre)
-    )
-    moved = lax.all_to_all(fourier, "gx", split_axis=2, concat_axis=3, tiled=True)
-    unmixed_values = jnp.einsum(
-        "frsl,sln->snfr",
-        lax.all_gather(moved, "gy", axis=0, tiled=True),
-        masked,
-        preferred_element_type=jnp.float32,
-    )
-    unmixed_values = unmixed_values.reshape(own_orders, own_degrees, variables, levels, 2)
-    mixed_tracer = jnp.einsum(
-        "hkz,fchzu->fchku", mixing, unmixed_values, precision=lax.Precision.HIGHEST
-    )
-    spectral = mixed_tracer.reshape(own_orders, own_degrees, variables * levels * 2)
+    spectral = spectral_part(forced, mixing, order_slot, legendre)
     sources = wind_source.reshape(bands, -1)
     slots = sources.shape[1]
     every_band = lax.all_gather(wind, "gx", axis=1, tiled=True)

time: 1360 us -> 1190 us (0.88)
  waiting for transfers between devices: 895 us -> 130 us
  Pallas kernels: 0 us -> 711 us
  matrix products: 101 us -> 38.9 us
  local copies, waits for them, and re-layouts: 203 us -> 164 us
  other arithmetic: 82.1 us -> 66.4 us
    pallas_call x0 -> x1, Pallas kernels: none -> 711 us  [spectral_part(): pl.pallas_call(functools.partial(spectral_kernel, nx, nz, chunks), out_sh...]
    all_gather x1 -> x0, waiting for transfers between devices: 654 us -> none  [shards(): lax.all_gather(moved, 'gy', axis=0, tiled=True)]
    all_to_all x1 -> x0, waiting for transfers between devices: 164 us -> none  [shards(): lax.all_to_all(fourier, 'gx', split_axis=2, concat_axis=3, tiled=True)]
    dot_general x3 -> x1, matrix products: 93.9 us -> 31.3 us  [spectral_part(): jnp.einsum('fal,lqp->paqf', forced, table.reshape(longitudes, 4, pairs),...]
    all_to_all x2 -> x0, local copies, waits for them, and re-layouts: 50.6 us -> none  [shards(): lax.all_to_all(fourier, 'gx', split_axis=2, concat_axis=3, tiled=True)]
    psum x1, waiting for transfers between devices: 0.02 us -> 40 us  [shards(): wind = lax.psum(partial_wind_stress.astype(jnp.bfloat16), 'gy')]
    unnamed x26 -> x31, local copies, waits for them, and re-layouts: 30.1 us -> 65.3 us
    transpose x1 -> x0, local copies, waits for them, and re-layouts: 34.3 us -> none  [shards(): jnp.einsum('hkz,fchzu->fchku', mixing, unmixed_values, precision=lax.Prec...]
  transfers between devices with their start and end apart: 22 -> 20, of which waited for: 14 -> 9; matrix products, arithmetic and copies ran while one was open for 13% -> 13% of each run, Pallas kernels for 0% -> 61%
where the time goes in v1:
time: 1190 us; the launch traced here: 1170 us
  Pallas kernels  711 us (60%)
  local copies, waits for them, and re-layouts  164 us (14%)
  waiting for transfers between devices  130 us (11%)
  other arithmetic  66.4 us (6%)
  starting transfers between devices  45.5 us (4%)
  matrix products  38.9 us (3%)
  between operations  14.7 us (1%)
    pallas_call x1, Pallas kernels, spectral_part(): pl.pallas_call(functools.partial(spectral_kernel, nx, nz, chunks), out_sh...  711 us
    unnamed x31, local copies, waits for them, and re-layouts  65.3 us
    reshape x2, local copies, waits for them, and re-layouts, spectral_part(): four = four.reshape(nx, chunks, PAIRS * band, 128)  49.5 us
    psum x1, waiting for transfers between devices, shards(): wind = lax.psum(partial_wind_stress.astype(jnp.bfloat16), 'gy')  40 us
    psum x1, waiting for transfers between devices, shards(): lax.psum(partial_surface, 'gy').reshape(band_rows, longitudes)  39 us
    dot_general x1, matrix products, spectral_part(): jnp.einsum('fal,lqp->paqf', forced, table.reshape(longitudes, 4, pairs),...  31.3 us
    all_gather x1, waiting for transfers between devices, shards(): every_band = lax.all_gather(wind, 'gx', axis=1, tiled=True)  30.3 us
    ppermute x8, starting transfers between devices, with_halo(): before = lax.ppermute(last, axis, up)  28.6 us
  transfers between devices with their start and end apart: 20, of which 9 were waited for; matrix products, arithmetic and copies ran while one was open for 13% of the time, Pallas kernels for 61%

profile of v1, /device:TPU:0, one launch (start us, length us, event | category | flops | bytes accessed | tf_op | source)
XLA Modules:
  0.0 1170.2 jit_solution(12782879291593410154)
XLA Ops:
  27.8 7.1 gather_fusion
  35.6 5.7 all-to-all-start
  41.4 4.6 all-to-all-done
  46.1 7.4 scatter_custom_fusion
  55.7 39.0 %all-reduce.4.cloned.1.call-done = f32[100,1600]{1,0:T(8,128)} async-done(((f32[100,1600]{1,0:T(8,128)}), f32[100,1600]{1,0:T(8,128)}) %all-reduce.4.cloned.1.call-update) | async-done | bytes 640016 | tf_op jit(solution)/shard_map/psum | solution.py:378
  94.7 6.8 add_convert_fusion
  105.5 10.4 copy.31
  115.9 12.6 %reshape.739 = bf16[32,160000]{1,0:T(8,128)(2,1)} reshape(bf16[32,100,1600]{2,1,0:T(8,128)(2,1)} %copy.31) | data formatting | bytes 20480000 | tf_op jit(solution)/shard_map/reshape | solution.py:388
  128.5 7.6 convolution_convert_fusion
  136.3 40.0 %all-reduce.6.cloned.1.call-done = bf16[2,160000]{1,0:T(2,128)(2,1)} async-done(((bf16[2,160000]{1,0:T(2,128)(2,1)}), bf16[2,160000]{1,0:T(2,128)(2,1)}) %all-reduce.6.cloned.1.call-update) | async-done | bytes 640016 | tf_op jit(solution)/shard_map/psum | solution.py:391
  177.3 8.0 negate_convert_fusion
  188.3 30.3 %all-gather.2.cloned.1.call-done = bf16[2,1280000]{1,0:T(2,128)(2,1)} async-done(((bf16[2,160000]{1,0:T(2,128)(2,1)}), bf16[2,1280000]{1,0:T(2,128)(2,1)}) %all-gather.2.cloned.1.call-update) | async-done | bytes 5120016 | tf_op jit(solution)/shard_map/all_gather | solution.py:395
  218.6 8.6 gather_fusion.1
  227.8 12.0 %scatter_custom_fusion.1 = f32[2,16384]{0,1:T(8,128)} fusion(s32[1280]{0:T(1024)S(1)} %fusion.110, f32[]{:T(128)} %constant.251.clone.1, f32[2,1280]{0,1:T(8,128)S(1)} %bitcast_multiply_fusion), kind=kCustom, calls=%fused_computation.29 | custom fusion | flops 2560 | bytes 786436 | tf_op jit(solution)/shard_map/scatter-add | solution.py:404
  239.8 10.4 fusion.6
  270.0 4.2 collective-permute-start.8
  294.3 5.3 collective-permute-start.12
  302.2 45.7 %copy.35.leg_ref = bf16[100,800,200]{2,1,0:T(8,128)(2,1)} copy(bf16[100,800,200]{1,2,0:T(8,128)(2,1)} %param.37) | data formatting | bytes 64000000 | tf_op args[4]
  348.1 4.3 collective-permute-start.14
  353.9 31.3 %convert_bitcast_fusion = bf16[416,100,4,32]{1,0,3,2:T(8,128)(2,1)} fusion(bf16[1600,4,416,1]{0,2,3,1:T(8,128)(2,1)} %bitcast.116, bf16[32,100,1600]{2,0,1:T(8,128)(2,1)} %copy-done.2), kind=kOutput, calls=%fused_computation.6 | convolution fusion | flops 17044684800 | bytes 26214400 | tf_op jit(solution)/shard_map/fal,lqp->paqf/dot_general | solution.py:277
  385.2 26.6 %reshape.737 = bf16[8,13,400,128]{2,1,0,3:T(8,128)(2,1)} reshape(bf16[416,100,4,32]{1,0,3,2:T(8,128)(2,1)} %convert_bitcast_fusion) | data formatting | bytes 21299200 | tf_op jit(solution)/shard_map/reshape | solution.py:280
  411.8 22.9 %copy.34.four_ref = bf16[8,13,400,128]{3,2,1,0:T(8,128)(2,1)} copy(bf16[8,13,400,128]{2,1,0,3:T(8,128)(2,1)} %reshape.737) | data formatting | bytes 21299200 | tf_op jit(solution)/shard_map/reshape | solution.py:280
  434.7 710.8 %shard_map.158 = f32[100,200,256]{2,1,0:T(8,128)} custom-call(bf16[8,13,400,128]{3,2,1,0:T(8,128)(2,1)} %copy.34.four_ref, bf16[100,800,200]{2,1,0:T(8,128)(2,1)} %copy.35.leg_ref, f32[2,512,256]{2,1,0:T(8,128)} %broadcast_multiply_fusion.mix_ref, s32[800]{0:T(1024)} %order_ref.1), custom_call_target="tpu_custom_call" | custom-call | tf_op jit(solution)/shard_map/pallas_call | solution.py:298
  1147.9 15.6 %copy.58 = f32[100,200,256]{2,1,0:T(8,128)} copy(f32[100,200,256]{2,1,0:T(8,128)} %shard_map.158) | data formatting | bytes 40960000
  (154 shorter events, 78.5 us)
Async XLA Ops:
  7.2 169.6 %copy-start = (s32[1,1,8]{2,1,0:T(1,128)S(1)}, s32[1,1,8]{2,1,0:T(1,128)}, u32[]{:S(2)}) copy-start(s32[1,1,8]{2,1,0:T(1,128)} %param.47) | copy-start | bytes 100
  9.2 4.5 collective-permute-start
  11.6 5.4 collective-permute-start.1
  17.3 5.6 collective-permute-start.2
  20.8 5.6 collective-permute-start.3
  27.8 66.9 %copy-start.13 = (f32[32]{0:T(128)S(1)}, f32[32]{0:T(128)}, u32[]{:S(2)}) copy-start(f32[32]{0:T(128)} %param.34) | copy-start | bytes 388
  35.6 10.4 all-to-all-start
  41.3 53.4 %all-reduce.4.cloned.1.call-start = ((), (), s32[]{:S(2)}) async-start(), calls=%async_computation.1 | async-start | bytes 1384448 | tf_op jit(solution)/shard_map/psum | solution.py:378
  54.6 121.8 %all-reduce.6.cloned.1.call-start = ((), (), s32[]{:S(2)}) async-start(), calls=%async_computation.2 | async-start | bytes 1280000 | tf_op jit(solution)/shard_map/psum | solution.py:391
  128.5 48.0 %copy-start.10 = (s32[1,1280]{1,0:T(1,128)S(1)}, s32[1,1280]{1,0:T(1,128)}, u32[]{:S(2)}) copy-start(s32[1,1280]{1,0:T(1,128)} %param.45) | copy-start | bytes 15364
  128.5 48.8 %copy-start.12 = (s32[1,1280]{1,0:T(1,128)S(1)}, s32[1,1280]{1,0:T(1,128)}, u32[]{:S(2)}) copy-start(s32[1,1280]{1,0:T(1,128)} %param.46) | copy-start | bytes 15364
  136.1 82.5 %all-gather.2.cloned.1.call-start = ((), (), s32[]{:S(2)}) async-start(), calls=%async_computation.3 | async-start | bytes 5760000 | tf_op jit(solution)/shard_map/all_gather | solution.py:395
  252.7 3.5 collective-permute-start.4
  254.9 4.1 collective-permute-start.5
  259.2 5.3 collective-permute-start.6
  262.7 5.6 collective-permute-start.7
  270.0 5.5 collective-permute-start.8
  274.2 4.0 collective-permute-start.9
  278.5 13.0 %collective-permute-start.10 = (bf16[9,1,258]{2,1,0:T(2,128)(2,1)S(1)}, bf16[9,1,258]{2,1,0:T(2,128)(2,1)S(1)}, u32[]{:S(2)}, u32[]{:S(2)}) collective-permute-start(bf16[9,1,258]{2,1,0:T(2,128)(2,1)S(1)} %get-tuple-element.136), channel_id=1, source_target_pairs={{0,1},{1,2},{2,3},{4,5},{5,6},{6,7},{8,9},{9,10},{10,11},{12,13},{... | collective-permute-start | bytes 13940 | tf_op jit(solution)/shard_map/ppermute | solution.py:25
  281.9 9.6 collective-permute-start.11
  294.3 53.5 %collective-permute-start.12 = (bf16[9,64,1]{2,1,0:T(8,128)(2,1)S(1)}, bf16[9,64,1]{2,1,0:T(8,128)(2,1)S(1)}, u32[]{:S(2)}, u32[]{:S(2)}) collective-permute-start(bf16[9,64,1]{2,1,0:T(8,128)(2,1)S(1)} %get-tuple-element.142), channel_id=1, source_target_pairs={{0,4},{4,8},{8,12},{12,16},{16,20},{20,24},{24,28},{1,5},{5,9},{9,... | collective-permute-start | bytes 3464 | tf_op jit(solution)/shard_map/ppermute | solution.py:25
  299.7 48.2 %collective-permute-start.13 = (bf16[9,64,1]{2,1,0:T(8,128)(2,1)S(1)}, bf16[9,64,1]{2,1,0:T(8,128)(2,1)S(1)}, u32[]{:S(2)}, u32[]{:S(2)}) collective-permute-start(bf16[9,64,1]{2,1,0:T(8,128)(2,1)S(1)} %get-tuple-element.143), channel_id=1, source_target_pairs={{4,0},{8,4},{12,8},{16,12},{20,16},{24,20},{28,24},{5,1},{9,5},{13... | collective-permute-start | bytes 3464 | tf_op jit(solution)/shard_map/ppermute | solution.py:26
  348.1 797.3 %collective-permute-start.14 = (bf16[9,1,258]{2,1,0:T(2,128)(2,1)S(1)}, bf16[9,1,258]{2,1,0:T(2,128)(2,1)S(1)}, u32[]{:S(2)}, u32[]{:S(2)}) collective-permute-start(bf16[9,1,258]{2,1,0:T(2,128)(2,1)S(1)} %get-tuple-element.134), channel_id=1, source_target_pairs={{0,1},{1,2},{2,3},{4,5},{5,6},{6,7},{8,9},{9,10},{10,11},{12,13},{... | collective-permute-start | bytes 13940 | tf_op jit(solution)/shard_map/ppermute | solution.py:25
  352.4 793.1 %collective-permute-start.15 = (bf16[9,1,258]{2,1,0:T(2,128)(2,1)S(1)}, bf16[9,1,258]{2,1,0:T(2,128)(2,1)S(1)}, u32[]{:S(2)}, u32[]{:S(2)}) collective-permute-start(bf16[9,1,258]{2,1,0:T(2,128)(2,1)S(1)} %get-tuple-element.135), channel_id=1, source_target_pairs={{1,0},{2,1},{3,2},{5,4},{6,5},{7,6},{9,8},{10,9},{11,10},{13,12},{... | collective-permute-start | bytes 13940 | tf_op jit(solution)/shard_map/ppermute | solution.py:26
  (10 other events, 157.6 us)
Sparse Core Ops, SparseCore 0:
  54.7 39.9 all-reduce.3
  136.2 40.1 all-reduce.5
  178.3 40.2 all-gather.1
